TPU v7x, 32 devices: a whole 2x2x4 slice. The times are simulated.
32 devices in a mesh: groups: 2 (over y), walker: 16 (over z, x, core).
Axes of the slice: x: 2, y: 2, z: 4, core: 2. Of those that a mesh axis runs over, the one named last changes fastest.
Arguments:
- log_grads: float32 [256, 2048], P(('groups', 'walker')), parts along dimension 0
- local_energy: float32 [256], P(('groups', 'walker')), parts along dimension 0
- prev_update: float32 [4096], P('groups'), parts along dimension 0, may hold values from -6 to 6
Outputs:
- kernel_rows: float32 [256, 128], P(('groups', 'walker')), parts along dimension 0
- coeffs: float32 [256], P(('groups', 'walker')), parts along dimension 0
- update: float32 [4096], P('groups'), parts along dimension 0
There are 2 independent parts, one for each index of `groups`. A program takes and returns all parts, laid end to end along the dimension named above; each array names one. Nothing has to cross between parts.
All inputs are finite; a program needn't handle non-finite values.
Results may differ from a plain program's by a relative error of at most 0.0015.
Values may be sent and summed in bfloat16 or wider, within the bound.
A program may use at most 64 MiB of HBM per device.

v0:
```python
import jax
import jax.numpy as jnp
from jax import lax
from jax.sharding import PartitionSpec as P

ITERS = 2


momentum = 0.9
damping = 0.5


def local(log_grads, local_energy, prev_update):
    high = lax.Precision.HIGHEST
    rows = log_grads.shape[0]
    count = rows * lax.axis_size("walker")
    col_sum, energy_sum = lax.psum((jnp.sum(log_grads, axis=0), jnp.sum(local_energy)), "walker")
    centered = (log_grads - col_sum / count) * count ** (-0.5)
    blocks = centered.astype(jnp.bfloat16)
    gathered = lax.all_gather(blocks, "walker", axis=0, tiled=True)
    kernel_rows = lax.dot_general(
        blocks, gathered, (((1,), (1,)), ((), ())), preferred_element_type=jnp.float32
    )
    target = -(local_energy - energy_sum / count) - momentum * jnp.dot(
        centered, prev_update, precision=high
    )
    coeffs = jnp.zeros_like(target)
    residual = target

    def squares(resid):
        return lax.psum(jnp.sum(resid * resid), "walker")

    direction = residual
    norm_now = squares(residual)
    for step in range(ITERS):
        full = lax.all_gather(direction, "walker", axis=0, tiled=True)
        image = jnp.dot(kernel_rows, full, precision=high) + damping * direction
        alpha = norm_now / lax.psum(jnp.sum(direction * image), "walker")
        coeffs = coeffs + alpha * direction
        if step + 1 < ITERS:
            residual = residual - alpha * image
            norm_next = squares(residual)
            direction = residual + norm_next / norm_now * direction
            norm_now = norm_next
    update = lax.psum(jnp.dot(coeffs, centered, precision=high), "walker") + momentum * prev_update
    return (kernel_rows, coeffs, update)


def solution(mesh):
    in_specs = (P(("groups", "walker"), None), P(("groups", "walker")), P("groups"))
    out_specs = (P(("groups", "walker"), None), P(("groups", "walker")), P("groups"))
    return jax.shard_map(local, mesh=mesh, in_specs=in_specs, out_specs=out_specs, check_vma=False)
```

profile of v0, /device:TPU:0, one launch (start us, length us, event | category | flops | bytes accessed | tf_op | source)
XLA Modules:
  0.0 249.6 jit_solution(12472072144584226088)
XLA Ops:
  0.6 0.0 copy-start
  0.6 0.0 copy-start.4
  0.6 0.9 reduce_sum.54
  1.6 0.0 copy-done.4
  1.6 0.6 reduce_sum.55
  2.2 36.6 %all-reduce.3 = (f32[2048]{0:T(1024)S(1)}, f32[]{:T(128)}) all-reduce(f32[2048]{0:T(1024)S(1)} %reduce_sum.54, f32[]{:T(128)} %reduce_sum.55), channel_id=1, replica_groups=mesh['groups'=2,'walker'=16] {'walker'}, use_global_device_ids=true, to_apply=%region_1.0 | all-reduce | flops 2049 | bytes 16392 | tf_op jit(solution)/shard_map/psum | solution.py:17
  38.7 0.0 copy-done
  38.8 18.7 %all_gather.9 = bf16[128,2048]{1,0:T(8,128)(2,1)S(1)} all-gather(bf16[8,2048]{1,0:T(8,128)(2,1)S(1)} %fusion.7), channel_id=1, replica_groups=mesh['groups'=2,'walker'=16] {'walker'}, dimensions={0}, use_global_device_ids=true | all-gather | bytes 557056 | tf_op jit(solution)/shard_map/all_gather | solution.py:20
  57.5 0.0 copy-start.1
  57.5 0.2 fusion.18
  57.7 0.0 copy-start.2
  58.4 0.0 copy-done.1
  58.4 0.2 fusion.1
  58.6 0.0 copy-start.5
  58.6 0.7 copy-done.5
  59.3 0.6 dynamic-slice
  60.6 0.2 dynamic-update-slice
  60.8 31.8 %all-reduce = f32[128]{0:T(128)S(1)} all-reduce(f32[128]{0:T(128)S(1)} %dynamic-update-slice), channel_id=1, replica_groups=mesh['groups'=2,'walker'=16] {'walker'}, use_global_device_ids=true, to_apply=%add | all-reduce | flops 128 | bytes 1024
  92.6 0.8 multiply_reduce_fusion.1
  93.4 30.1 %all-reduce.2 = (f32[]{:T(128)}, f32[]{:T(128)}) all-reduce(f32[]{:T(128)} %get-tuple-element.4, f32[]{:T(128)} %get-tuple-element.3), channel_id=1, replica_groups=mesh['groups'=2,'walker'=16] {'walker'}, use_global_device_ids=true, to_apply=%region_5.0 | all-reduce | flops 2 | bytes 16 | tf_op jit(solution)/shard_map/psum | solution.py:31
  124.8 0.6 multiply_reduce_fusion
  125.4 30.1 %psum.53 = f32[]{:T(128)} all-reduce(f32[]{:T(128)} %multiply_reduce_fusion), channel_id=1, replica_groups=mesh['groups'=2,'walker'=16] {'walker'}, use_global_device_ids=true, to_apply=%region_9.0 | all-reduce | flops 1 | bytes 8 | tf_op jit(solution)/shard_map/psum | solution.py:31
  156.8 0.1 fusion.17
  156.9 29.5 %all-reduce.1 = f32[128]{0:T(128)S(1)} all-reduce(f32[128]{0:T(128)S(1)} %get-tuple-element.9), channel_id=1, replica_groups=mesh['groups'=2,'walker'=16] {'walker'}, use_global_device_ids=true, to_apply=%add.1 | all-reduce | flops 128 | bytes 1024
  186.3 0.0 copy-done.2
  186.3 0.7 fusion.5
  187.1 30.1 %psum.54 = f32[]{:T(128)} all-reduce(f32[]{:T(128)} %fusion.5), channel_id=1, replica_groups=mesh['groups'=2,'walker'=16] {'walker'}, use_global_device_ids=true, to_apply=%region_11.0 | all-reduce | flops 1 | bytes 8 | tf_op jit(solution)/shard_map/psum | solution.py:38
  218.5 0.0 copy-start.3
  218.5 0.2 fusion.6
  218.7 0.3 copy-done.3
  219.1 30.0 %psum.55 = f32[2048]{0:T(1024)S(1)} all-reduce(f32[2048]{0:T(1024)S(1)} %bitcast.37), channel_id=1, replica_groups=mesh['groups'=2,'walker'=16] {'walker'}, use_global_device_ids=true, to_apply=%region_12.0 | all-reduce | flops 2048 | bytes 16384 | tf_op jit(solution)/shard_map/psum | solution.py:45
  249.0 0.6 multiply_add_fusion
  (5 shorter events, 0.0 us)
Async XLA Ops:
  0.6 38.1 %copy-start = (f32[8,2048]{1,0:T(8,128)S(1)}, f32[8,2048]{1,0:T(8,128)}, u32[]{:S(2)}) copy-start(f32[8,2048]{1,0:T(8,128)} %param.3) | copy-start | bytes 196612
  0.6 0.9 copy-start.4
  57.5 0.9 copy-start.1
  57.7 128.6 %copy-start.2 = (f32[8,128]{1,0:T(8,128)}, f32[8,128]{1,0:T(8,128)S(1)}, u32[]{:S(2)}) copy-start(f32[8,128]{1,0:T(8,128)S(1)} %fusion.18) | copy-start | bytes 12292
  58.6 0.7 copy-start.5
  218.5 0.5 copy-start.3
where the time goes:
time: 250 us
  blocking collectives  237 us (95%)
  between operations  5.89 us (2%)
  other arithmetic  2.84 us (1%)
    unnamed x2, blocking collectives  61.3 us
    psum x2, blocking collectives, squares(): return lax.psum(jnp.sum(resid * resid), 'walker')  60.2 us
    psum x1, blocking collectives, local(): lax.psum((jnp.sum(log_grads, axis=0), jnp.sum(local_energy)), 'walker')  36.6 us
    psum x1, blocking collectives, local(): alpha = norm_now / lax.psum(jnp.sum(direction * image), 'walker')  30.1 us
    psum x1, blocking collectives, local(): lax.psum(jnp.dot(coeffs, centered, precision=high), 'walker')  30 us
    all_gather x1, blocking collectives, local(): gathered = lax.all_gather(blocks, 'walker', axis=0, tiled=True)  18.7 us

commit v1 on v0

--- a/solution.py
+++ b/solution.py
@@ -1,16 +1,181 @@
+import functools
+
 import jax
 import jax.numpy as jnp
 from jax import lax
+from jax.experimental import pallas as pl
+from jax.experimental.pallas import tpu as pltpu
 from jax.sharding import PartitionSpec as P
 
 ITERS = 2
-
+LANES = 128
+ROWS = 8
+MESH = pl.DeviceIdType.MESH
 
 momentum = 0.9
 damping = 0.5
 
 
-def local(log_grads, local_energy, prev_update):
+def kernel(
+    n, x_hbm, e_hbm, p_hbm, rows_ref, coeffs_ref, update_ref,
+    x_ref, e_ref, p_ref, tiles, w_rows, y_rows, k_send, k_recv, fin,
+    in_sem, send_sem, recv_sem,
+):
+    walkers = n * ROWS
+    scale = walkers ** (-0.5)
+    group = lax.axis_index("groups")
+    me = lax.axis_index("walker")
+    peers = [lax.rem(me + k, n) for k in range(n - 1, 0, -1)]
+
+    barrier = pltpu.get_barrier_semaphore()
+    for peer in peers:
+        pl.semaphore_signal(barrier, inc=1, device_id=(group, peer), device_id_type=MESH)
+    loads = [
+        pltpu.make_async_copy(x_hbm, x_ref, in_sem.at[0]),
+        pltpu.make_async_copy(p_hbm, p_ref, in_sem.at[1]),
+        pltpu.make_async_copy(e_hbm, e_ref, in_sem.at[2]),
+    ]
+    for load in loads:
+        load.start()
+    for load in loads:
+        load.wait()
+
+    def column_tile(peer):
+        return x_ref.at[:, pl.ds(pl.multiple_of(peer * LANES, LANES), LANES)]
+
+    def remote(src, dst, which, peer):
+        return pltpu.make_async_remote_copy(
+            src_ref=src, dst_ref=dst, send_sem=send_sem.at[which], recv_sem=recv_sem.at[which],
+            device_id=(group, peer), device_id_type=MESH,
+        )
+
+    def arrived(ref, which):
+        part = ref.at[pl.ds(0, n - 1)]
+        pltpu.make_async_copy(part, part, recv_sem.at[which]).wait()
+
+    def sent(ref, which):
+        part = ref.at[pl.ds(0, n - 1)]
+        pltpu.make_async_copy(part, part, send_sem.at[which]).wait()
+
+    lane = lax.broadcasted_iota(jnp.int32, (1, LANES), 1)
+    lane8 = lax.broadcasted_iota(jnp.int32, (ROWS, LANES), 1)
+    sub8 = lax.broadcasted_iota(jnp.int32, (ROWS, LANES), 0)
+
+    acc = jnp.zeros((ROWS, LANES), jnp.float32)
+    for k in range(n):
+        acc = acc + x_ref[:, k * LANES : (k + 1) * LANES] * p_ref[k : k + 1, :]
+    own = jnp.sum(acc, axis=1, keepdims=True) * (-momentum * scale)
+    w_row = jnp.sum(jnp.where(lane8 == me * ROWS + sub8, own, 0.0), axis=0, keepdims=True)
+    for i in range(ROWS):
+        w_row = w_row - jnp.where(lane == me * ROWS + i, e_ref[i], 0.0)
+    w_rows[me] = w_row
+    tiles[me] = x_ref[:, pl.ds(pl.multiple_of(me * LANES, LANES), LANES)]
+
+    pl.semaphore_wait(barrier, n - 1)
+    for peer in peers:
+        remote(column_tile(peer), tiles.at[me], 0, peer).start()
+        remote(w_rows.at[me], w_rows.at[me], 1, peer).start()
+
+    sub = lax.broadcasted_iota(jnp.int32, (walkers, LANES), 0)
+    lanes = lax.broadcasted_iota(jnp.int32, (walkers, LANES), 1)
+    diagonal = sub == lanes
+
+    def to_column(row):
+        return jnp.sum(jnp.where(diagonal, row, 0.0), axis=1, keepdims=True)
+
+    def to_row(column):
+        return jnp.sum(jnp.where(diagonal, column, 0.0), axis=0, keepdims=True)
+
+    arrived(w_rows, 1)
+    w = jnp.sum(w_rows[...], axis=0)
+    t = w - jnp.sum(w, axis=1, keepdims=True) / walkers
+    t_col = to_column(t)
+    arrived(tiles, 0)
+    x = tiles[...].reshape(walkers, LANES)
+    centered = (x - jnp.sum(x, axis=0, keepdims=True) / walkers) * scale
+    half = centered.astype(jnp.bfloat16)
+    blocks = half.astype(jnp.float32)
+    bt = jnp.sum(blocks * t_col, axis=0, keepdims=True)
+    y_rows[me] = to_row(jnp.sum(blocks * bt, axis=1, keepdims=True))
+    for peer in peers:
+        remote(y_rows.at[me], y_rows.at[me], 2, peer).start()
+
+    k_part = lax.dot_general(half, half, (((1,), (1,)), ((), ())), preferred_element_type=jnp.float32)
+    k_send[...] = k_part.reshape(n, ROWS, LANES)
+    k_recv[me] = k_send[me]
+    for peer in peers:
+        remote(k_send.at[peer], k_recv.at[me], 3, peer).start()
+    ct = jnp.sum(centered * t_col, axis=0, keepdims=True)
+    norm = jnp.sum(t * t, axis=1, keepdims=True)
+
+    arrived(y_rows, 2)
+    image = jnp.sum(y_rows[...], axis=0) + damping * t
+    alpha = norm / jnp.sum(t * image, axis=1, keepdims=True)
+    residual = t - alpha * image
+    norm_next = jnp.sum(residual * residual, axis=1, keepdims=True)
+    direction = residual + norm_next / norm * t
+    d_col = to_column(direction)
+    bd = jnp.sum(blocks * d_col, axis=0, keepdims=True)
+    cd = jnp.sum(centered * d_col, axis=0, keepdims=True)
+    fin[me, :, 0:LANES] = alpha * ct + momentum * p_ref[pl.ds(me, 1), :]
+    fin[me, :, LANES : 2 * LANES] = cd
+    fin[me, :, 2 * LANES : 3 * LANES] = bd * bd
+    for peer in peers:
+        remote(fin.at[me], fin.at[me], 4, peer).start()
+
+    square = jnp.sum(direction * direction, axis=1, keepdims=True)
+    arrived(k_recv, 3)
+    rows_ref[...] = jnp.sum(k_recv[...], axis=0)
+
+    arrived(fin, 4)
+    curve = jnp.sum(jnp.sum(fin[:, :, 2 * LANES : 3 * LANES], axis=0), axis=1, keepdims=True)
+    alpha2 = norm_next / (curve + damping * square)
+    coeffs = alpha * t + alpha2 * direction
+    coeffs_ref[...] = jnp.broadcast_to(
+        jnp.sum(jnp.where(lane8 == me * ROWS + sub8, coeffs, 0.0), axis=1, keepdims=True), (ROWS, LANES)
+    )
+    for k in range(n):
+        update_ref[k : k + 1, :] = fin[k, :, 0:LANES] + alpha2 * fin[k, :, LANES : 2 * LANES]
+
+    sent(tiles, 0)
+    sent(w_rows, 1)
+    sent(y_rows, 2)
+    sent(k_recv, 3)
+    sent(fin, 4)
+
+
+def fused(log_grads, local_energy, prev_update):
+    n = lax.axis_size("walker")
+    f32 = jnp.float32
+    rows, coeffs, update = pl.pallas_call(
+        functools.partial(kernel, n),
+        out_shape=(
+            jax.ShapeDtypeStruct((ROWS, LANES), f32),
+            jax.ShapeDtypeStruct((ROWS, LANES), f32),
+            jax.ShapeDtypeStruct((n, LANES), f32),
+        ),
+        in_specs=[pl.BlockSpec(memory_space=pl.ANY)] * 3,
+        out_specs=[pl.BlockSpec(memory_space=pltpu.VMEM)] * 3,
+        scratch_shapes=[
+            pltpu.VMEM((ROWS, n * LANES), f32),
+            pltpu.SMEM((ROWS,), f32),
+            pltpu.VMEM((n, LANES), f32),
+            pltpu.VMEM((n, ROWS, LANES), f32),
+            pltpu.VMEM((n, 1, LANES), f32),
+            pltpu.VMEM((n, 1, LANES), f32),
+            pltpu.VMEM((n, ROWS, LANES), f32),
+            pltpu.VMEM((n, ROWS, LANES), f32),
+            pltpu.VMEM((n, 1, 3 * LANES), f32),
+            pltpu.SemaphoreType.DMA((3,)),
+            pltpu.SemaphoreType.DMA((5,)),
+            pltpu.SemaphoreType.DMA((5,)),
+        ],
+        compiler_params=pltpu.CompilerParams(collective_id=0, has_side_effects=True),
+    )(log_grads, local_energy, prev_update.reshape(n, LANES))
+    return rows, coeffs[:, 0], update.reshape(n * LANES)
+
+
+def plain(log_grads, local_energy, prev_update):
     high = lax.Precision.HIGHEST
     rows = log_grads.shape[0]
     count = rows * lax.axis_size("walker")
@@ -46,6 +211,14 @@
     return (kernel_rows, coeffs, update)
 
 
+def local(log_grads, local_energy, prev_update):
+    rows, columns = log_grads.shape
+    n = lax.axis_size("walker")
+    if rows == ROWS and n * ROWS == LANES and columns == n * LANES:
+        return fused(log_grads, local_energy, prev_update)
+    return plain(log_grads, local_energy, prev_update)
+
+
 def solution(mesh):
     in_specs = (P(("groups", "walker"), None), P(("groups", "walker")), P("groups"))
     out_specs = (P(("groups", "walker"), None), P(("groups", "walker")), P("groups"))

time: 250 us -> 22.2 us (0.09)
  blocking collectives: 237 us -> 0 us
  Pallas kernels: 0 us -> 18.8 us
  between operations: 5.89 us -> 0.66 us
  other arithmetic: 2.84 us -> 0 us
    psum x5 -> x0, blocking collectives: 157 us -> none  [the longest x2 60.2 us: squares(): return lax.psum(jnp.sum(resid * resid), 'walker')]
    unnamed x2 -> x0, blocking collectives: 61.3 us -> none
    pallas_call x0 -> x1, Pallas kernels: none -> 18.8 us  [fused(): pl.pallas_call(functools.partial(kernel, n), out_shape=(jax.ShapeDtypeStr...]
    all_gather x1 -> x0, blocking collectives: 18.7 us -> none  [local(): gathered = lax.all_gather(blocks, 'walker', axis=0, tiled=True)]
where the time goes in v1:
time: 22.2 us; the launch traced here: 22 us
  Pallas kernels  18.8 us (85%)
  local copies, waits for them, and re-layouts  2.47 us (11%)
  between operations  0.66 us (3%)
    pallas_call x1, Pallas kernels, fused(): pl.pallas_call(functools.partial(kernel, n), out_shape=(jax.ShapeDtypeStr...  18.8 us
    unnamed x8, local copies, waits for them, and re-layouts  1.85 us
    slice x1, local copies, waits for them, and re-layouts, fused(): return (rows, coeffs[:, 0], update.reshape(n * LANES))  0.62 us

profile of v1, /device:TPU:0, one launch (start us, length us, event | category | flops | bytes accessed | tf_op | source)
XLA Modules:
  0.0 22.0 jit_solution(16481264748857320653)
XLA Ops:
  0.6 18.8 %shard_map.58 = (f32[8,128]{1,0:T(8,128)}, f32[8,128]{1,0:T(8,128)}, f32[16,128]{1,0:T(8,128)}) custom-call(f32[8,2048]{1,0:T(8,128)} %x_hbm.1, f32[8]{0:T(128)} %e_hbm.1, f32[16,128]{1,0:T(8,128)} %bitcast.2), custom_call_target="tpu_custom_call" | custom-call | tf_op jit(solution)/shard_map/pallas_call | solution.py:150
  19.5 0.0 copy-start.1
  19.5 0.0 copy-start.2
  19.5 0.0 copy-start
  19.5 0.6 %copy-done.1 = f32[8,128]{1,0:T(8,128)S(1)} copy-done((f32[8,128]{1,0:T(8,128)S(1)}, f32[8,128]{1,0:T(8,128)}, u32[]{:S(2)}) %copy-start.1) | copy-done | bytes 4120
  20.2 0.6 %slice_reduce_fusion = f32[8]{0:T(128)} fusion(f32[8,128]{1,0:T(8,128)S(1)} %copy-done.1), kind=kLoop, calls=%fused_computation | loop fusion | bytes 64 | tf_op jit(solution)/shard_map/slice | solution.py:175
  20.8 0.0 copy-done.2
  20.8 0.6 %copy.8 = f32[8,128]{1,0:T(8,128)} copy(f32[8,128]{1,0:T(8,128)S(1)} %copy-done.2) | data formatting | bytes 8192
  21.4 0.0 copy-done
  21.4 0.6 %copy.9 = f32[2048]{0:T(1024)} copy(f32[2048]{0:T(1024)S(1)} %bitcast.3) | data formatting | bytes 16384
Async XLA Ops:
  19.5 0.7 %copy-start.1 = (f32[8,128]{1,0:T(8,128)S(1)}, f32[8,128]{1,0:T(8,128)}, u32[]{:S(2)}) copy-start(f32[8,128]{1,0:T(8,128)} %get-tuple-element.7) | copy-start | bytes 12292
  19.5 1.3 %copy-start.2 = (f32[8,128]{1,0:T(8,128)S(1)}, f32[8,128]{1,0:T(8,128)}, u32[]{:S(2)}) copy-start(f32[8,128]{1,0:T(8,128)} %get-tuple-element.12) | copy-start | bytes 12292
  19.5 1.9 %copy-start = (f32[16,128]{1,0:T(8,128)S(1)}, f32[16,128]{1,0:T(8,128)}, u32[]{:S(2)}) copy-start(f32[16,128]{1,0:T(8,128)} %get-tuple-element.8) | copy-start | bytes 24580

commit v2 on v1

v2 whole, which is shorter than its diff:
```python
import functools

import jax
import jax.numpy as jnp
from jax import lax
from jax.experimental import pallas as pl
from jax.experimental.pallas import tpu as pltpu
from jax.sharding import PartitionSpec as P

ITERS = 2
LANES = 128
ROWS = 8
TEAM = 8
MESH = pl.DeviceIdType.MESH

momentum = 0.9
damping = 0.5


def kernel(
    n, m, x_hbm, e_hbm, p_hbm, rows_ref, coeffs_ref, update_ref,
    x_ref, e_ref, p_ref, tiles, w_rows, y_rows, k_send, k_recv, fin,
    in_sem, send_sem, recv_sem,
):
    walkers = n * ROWS
    width = tiles.shape[2]
    chunks = width // LANES
    scale = walkers ** (-0.5)
    group = lax.axis_index("groups")
    me = lax.axis_index("walker")
    pos = lax.rem(me, m)
    team = me - pos
    peers = [lax.rem(me + k, n) for k in range(n - 1, 0, -1)]
    mates = [lax.rem(pos + k, m) for k in range(m - 1, 0, -1)]

    barrier = pltpu.get_barrier_semaphore()
    for peer in peers:
        pl.semaphore_signal(barrier, inc=1, device_id=(group, peer), device_id_type=MESH)
    loads = [
        pltpu.make_async_copy(x_hbm, x_ref, in_sem.at[0]),
        pltpu.make_async_copy(p_hbm, p_ref, in_sem.at[1]),
        pltpu.make_async_copy(e_hbm, e_ref, in_sem.at[2]),
    ]
    for load in loads:
        load.start()
    for load in loads:
        load.wait()

    def share(place):
        return pl.ds(pl.multiple_of(place * width, LANES), width)

    def remote(src, dst, which, peer):
        return pltpu.make_async_remote_copy(
            src_ref=src, dst_ref=dst, send_sem=send_sem.at[which], recv_sem=recv_sem.at[which],
            device_id=(group, peer), device_id_type=MESH,
        )

    def wait_all(ref, count, sem):
        if count:
            part = ref.at[pl.ds(0, count)]
            pltpu.make_async_copy(part, part, sem).wait()

    lane = lax.broadcasted_iota(jnp.int32, (1, LANES), 1)
    lane8 = lax.broadcasted_iota(jnp.int32, (ROWS, LANES), 1)
    sub8 = lax.broadcasted_iota(jnp.int32, (ROWS, LANES), 0)

    acc = jnp.zeros((ROWS, LANES), jnp.float32)
    for k in range(p_ref.shape[0]):
        acc = acc + x_ref[:, k * LANES : (k + 1) * LANES] * p_ref[k : k + 1, :]
    own = jnp.sum(acc, axis=1, keepdims=True) * (-momentum * scale)
    w_row = jnp.sum(jnp.where(lane8 == me * ROWS + sub8, own, 0.0), axis=0, keepdims=True)
    for i in range(ROWS):
        w_row = w_row - jnp.where(lane == me * ROWS + i, e_ref[i], 0.0)
    w_rows[me] = w_row
    tiles[me] = x_ref[:, share(pos)]

    pl.semaphore_wait(barrier, n - 1)
    for peer in peers:
        remote(w_rows.at[me], w_rows.at[me], 1, peer).start()
        remote(x_ref.at[:, share(lax.rem(peer, m))], tiles.at[me], 0, peer).start()

    sub = lax.broadcasted_iota(jnp.int32, (walkers, LANES), 0)
    lanes = lax.broadcasted_iota(jnp.int32, (walkers, LANES), 1)
    diagonal = sub == lanes

    def to_column(row):
        return jnp.sum(jnp.where(diagonal, row, 0.0), axis=1, keepdims=True)

    def to_row(column):
        return jnp.sum(jnp.where(diagonal, column, 0.0), axis=0, keepdims=True)

    def cols(c):
        return slice(c * LANES, (c + 1) * LANES)

    def rounded(c):
        return tiles[:, :, cols(c)].reshape(walkers, LANES).astype(jnp.bfloat16).astype(jnp.float32)

    wait_all(w_rows, n - 1, recv_sem.at[1])
    w = jnp.sum(w_rows[...], axis=0)
    t = w - jnp.sum(w, axis=1, keepdims=True) / walkers
    t_col = to_column(t)
    wait_all(tiles, n - 1, recv_sem.at[0])
    y_acc = jnp.zeros((walkers, LANES), jnp.float32)
    bt = []
    for c in range(chunks):
        x = tiles[:, :, cols(c)].reshape(walkers, LANES)
        centered = (x - jnp.sum(x, axis=0, keepdims=True) / walkers) * scale
        tiles[:, :, cols(c)] = centered.reshape(n, ROWS, LANES)
        blocks = centered.astype(jnp.bfloat16).astype(jnp.float32)
        bt.append(jnp.sum(blocks * t_col, axis=0, keepdims=True))
        y_acc = y_acc + blocks * bt[c]
    y_rows[pos] = to_row(jnp.sum(y_acc, axis=1, keepdims=True))
    for mate in mates:
        remote(y_rows.at[pos], y_rows.at[pos], 2, team + mate).start()

    half = tiles[...].reshape(walkers, width).astype(jnp.bfloat16)
    ours = tiles[pl.ds(team, m)].reshape(m * ROWS, width).astype(jnp.bfloat16)
    k_part = lax.dot_general(ours, half, (((1,), (1,)), ((), ())), preferred_element_type=jnp.float32)
    k_send[...] = k_part.reshape(m, ROWS, LANES)
    k_recv[pos] = k_send[pos]
    for mate in mates:
        remote(k_send.at[mate], k_recv.at[pos], 3, team + mate).start()
    ct = [
        jnp.sum(tiles[:, :, cols(c)].reshape(walkers, LANES) * t_col, axis=0, keepdims=True)
        for c in range(chunks)
    ]
    norm = jnp.sum(t * t, axis=1, keepdims=True)

    wait_all(y_rows, m - 1, recv_sem.at[2])
    image = jnp.sum(y_rows[...], axis=0) + damping * t
    i_col = to_column(image)
    alpha = norm / jnp.sum(t * image, axis=1, keepdims=True)
    residual = t - alpha * image
    norm_next = jnp.sum(residual * residual, axis=1, keepdims=True)
    beta = norm_next / norm
    direction = residual + beta * t
    squares = jnp.zeros((1, LANES), jnp.float32)
    for c in range(chunks):
        bi = jnp.sum(rounded(c) * i_col, axis=0, keepdims=True)
        ci = jnp.sum(tiles[:, :, cols(c)].reshape(walkers, LANES) * i_col, axis=0, keepdims=True)
        bd = (bt[c] - alpha * bi) + beta * bt[c]
        squares = squares + bd * bd
        fin[pos, :, cols(c)] = alpha * ct[c] + momentum * p_ref[pl.ds(pos * chunks + c, 1), :]
        fin[pos, :, cols(chunks + c)] = (ct[c] - alpha * ci) + beta * ct[c]
    fin[pos, :, cols(2 * chunks)] = squares
    for mate in mates:
        remote(fin.at[pos], fin.at[pos], 4, team + mate).start()

    square = jnp.sum(direction * direction, axis=1, keepdims=True)
    wait_all(k_recv, m - 1, recv_sem.at[3])
    rows_ref[...] = jnp.sum(k_recv[...], axis=0)

    wait_all(fin, m - 1, recv_sem.at[4])
    curve = jnp.sum(jnp.sum(fin[:, :, cols(2 * chunks)], axis=0), axis=1, keepdims=True)
    alpha2 = norm_next / (curve + damping * square)
    coeffs = alpha * t + alpha2 * direction
    coeffs_ref[...] = pltpu.roll(coeffs, lax.rem(walkers - me * ROWS, walkers), 1)
    for k in range(m * chunks):
        owner, c = k // chunks, k % chunks
        update_ref[k : k + 1, :] = fin[owner, :, cols(c)] + alpha2 * fin[owner, :, cols(chunks + c)]

    wait_all(tiles, n - 1, send_sem.at[0])
    wait_all(w_rows, n - 1, send_sem.at[1])
    wait_all(y_rows, m - 1, send_sem.at[2])
    wait_all(k_recv, m - 1, send_sem.at[3])
    wait_all(fin, m - 1, send_sem.at[4])


def finish(rows_in, coeffs_in, update_in, rows_ref, coeffs_ref, update_ref):
    rows_ref[...] = rows_in[...]
    coeffs_ref[...] = coeffs_in[0, 0:ROWS]
    update_ref[...] = update_in[...]


def fused(log_grads, local_energy, prev_update):
    n = lax.axis_size("walker")
    m = TEAM
    size = prev_update.shape[0]
    width = size // m
    f32 = jnp.float32
    rows, coeffs, update = pl.pallas_call(
        functools.partial(kernel, n, m),
        out_shape=(
            jax.ShapeDtypeStruct((ROWS, LANES), f32),
            jax.ShapeDtypeStruct((1, LANES), f32),
            jax.ShapeDtypeStruct((size // LANES, LANES), f32),
        ),
        in_specs=[pl.BlockSpec(memory_space=pl.ANY)] * 3,
        out_specs=[pl.BlockSpec(memory_space=pltpu.VMEM)] * 3,
        scratch_shapes=[
            pltpu.VMEM((ROWS, size), f32),
            pltpu.SMEM((ROWS,), f32),
            pltpu.VMEM((size // LANES, LANES), f32),
            pltpu.VMEM((n, ROWS, width), f32),
            pltpu.VMEM((n, 1, LANES), f32),
            pltpu.VMEM((m, 1, LANES), f32),
            pltpu.VMEM((m, ROWS, LANES), f32),
            pltpu.VMEM((m, ROWS, LANES), f32),
            pltpu.VMEM((m, 1, 2 * width + LANES), f32),
            pltpu.SemaphoreType.DMA((3,)),
            pltpu.SemaphoreType.DMA((5,)),
            pltpu.SemaphoreType.DMA((5,)),
        ],
        compiler_params=pltpu.CompilerParams(collective_id=0, has_side_effects=True),
    )(log_grads, local_energy, prev_update.reshape(size // LANES, LANES))
    rows, coeffs, update = pl.pallas_call(
        finish,
        out_shape=(
            jax.ShapeDtypeStruct((ROWS, LANES), f32),
            jax.ShapeDtypeStruct((ROWS,), f32),
            jax.ShapeDtypeStruct((size // LANES, LANES), f32),
        ),
        in_specs=[pl.BlockSpec(memory_space=pltpu.VMEM)] * 3,
        out_specs=[pl.BlockSpec(memory_space=pltpu.VMEM)] * 3,
    )(rows, coeffs, update)
    return rows, coeffs, update.reshape(size)


def plain(log_grads, local_energy, prev_update):
    high = lax.Precision.HIGHEST
    rows = log_grads.shape[0]
    count = rows * lax.axis_size("walker")
    col_sum, energy_sum = lax.psum((jnp.sum(log_grads, axis=0), jnp.sum(local_energy)), "walker")
    centered = (log_grads - col_sum / count) * count ** (-0.5)
    blocks = centered.astype(jnp.bfloat16)
    gathered = lax.all_gather(blocks, "walker", axis=0, tiled=True)
    kernel_rows = lax.dot_general(
        blocks, gathered, (((1,), (1,)), ((), ())), preferred_element_type=jnp.float32
    )
    target = -(local_energy - energy_sum / count) - momentum * jnp.dot(
        centered, prev_update, precision=high
    )
    coeffs = jnp.zeros_like(target)
    residual = target

    def squares(resid):
        return lax.psum(jnp.sum(resid * resid), "walker")

    direction = residual
    norm_now = squares(residual)
    for step in range(ITERS):
        full = lax.all_gather(direction, "walker", axis=0, tiled=True)
        image = jnp.dot(kernel_rows, full, precision=high) + damping * direction
        alpha = norm_now / lax.psum(jnp.sum(direction * image), "walker")
        coeffs = coeffs + alpha * direction
        if step + 1 < ITERS:
            residual = residual - alpha * image
            norm_next = squares(residual)
            direction = residual + norm_next / norm_now * direction
            norm_now = norm_next
    update = lax.psum(jnp.dot(coeffs, centered, precision=high), "walker") + momentum * prev_update
    return (kernel_rows, coeffs, update)


def local(log_grads, local_energy, prev_update):
    rows, columns = log_grads.shape
    n = lax.axis_size("walker")
    if rows == ROWS and n * ROWS == LANES and columns == n * LANES:
        return fused(log_grads, local_energy, prev_update)
    return plain(log_grads, local_energy, prev_update)


def solution(mesh):
    in_specs = (P(("groups", "walker"), None), P(("groups", "walker")), P("groups"))
    out_specs = (P(("groups", "walker"), None), P(("groups", "walker")), P("groups"))
    return jax.shard_map(local, mesh=mesh, in_specs=in_specs, out_specs=out_specs, check_vma=False)
```

time: 22.2 us -> 20.2 us (0.910)
  local copies, waits for them, and re-layouts: 2.47 us -> 0 us
  Pallas kernels: 18.8 us -> 19.3 us
    unnamed x8 -> x0, local copies, waits for them, and re-layouts: 1.85 us -> none
    slice x1 -> x0, local copies, waits for them, and re-layouts: 0.62 us -> none  [fused(): return (rows, coeffs[:, 0], update.reshape(n * LANES))]
    pallas_call x1 -> x2, Pallas kernels: 18.8 us -> 19.3 us  [the longest x1 18 us: fused(): pl.pallas_call(functools.partial(kernel, n, m), out_shape=(jax.ShapeDtype...]
where the time goes in v2:
time: 20.2 us; the launch traced here: 20 us
  Pallas kernels  19.3 us (96%)
  between operations  0.64 us (3%)
    pallas_call x1, Pallas kernels, fused(): pl.pallas_call(functools.partial(kernel, n, m), out_shape=(jax.ShapeDtype...  18 us
    pallas_call x1, Pallas kernels, fused(): pl.pallas_call(finish, out_shape=(jax.ShapeDtypeStruct((ROWS, LANES), f32...  1.32 us

profile of v2, /device:TPU:0, one launch (start us, length us, event | category | flops | bytes accessed | tf_op | source)
XLA Modules:
  0.0 20.0 jit_solution(7435457614214569480)
XLA Ops:
  0.6 18.0 %shard_map.58 = (f32[8,128]{1,0:T(8,128)}, f32[1,128]{1,0:T(1,128)}, f32[16,128]{1,0:T(8,128)}) custom-call(f32[8,2048]{1,0:T(8,128)} %x_hbm.1, f32[8]{0:T(128)} %e_hbm.1, f32[16,128]{1,0:T(8,128)} %bitcast.2), custom_call_target="tpu_custom_call" | custom-call | tf_op jit(solution)/shard_map/pallas_call | solution.py:181
  18.6 1.3 %shard_map.59 = (f32[8,128]{1,0:T(8,128)}, f32[8]{0:T(128)}, f32[16,128]{1,0:T(8,128)}) custom-call(f32[8,128]{1,0:T(8,128)} %get-tuple-element.9.rows_in, f32[1,128]{1,0:T(1,128)} %get-tuple-element.10.coeffs_in, f32[16,128]{1,0:T(8,128)} %get-tuple-element.11.update_in), custom_call_target="tpu_custom_call" | custom-call | tf_op jit(solution)/shard_map/pallas_call | solution.py:206

commit v3 on v2

--- a/solution.py
+++ b/solution.py
@@ -30,11 +30,11 @@
     me = lax.axis_index("walker")
     pos = lax.rem(me, m)
     team = me - pos
-    peers = [lax.rem(me + k, n) for k in range(n - 1, 0, -1)]
-    mates = [lax.rem(pos + k, m) for k in range(m - 1, 0, -1)]
+    peers = [lax.rem(me + k, n) for k in range(1, n)]
+    mates = [lax.rem(pos + k, m) for k in range(1, m)]
 
     barrier = pltpu.get_barrier_semaphore()
-    for peer in peers:
+    for peer in peers[::-1]:
         pl.semaphore_signal(barrier, inc=1, device_id=(group, peer), device_id_type=MESH)
     loads = [
         pltpu.make_async_copy(x_hbm, x_ref, in_sem.at[0]),

time: 20.2 us -> 19.1 us (0.946)
  Pallas kernels: 19.3 us -> 18.3 us
    pallas_call x1, Pallas kernels: 18 us -> 16.9 us  [fused(): pl.pallas_call(functools.partial(kernel, n, m), out_shape=(jax.ShapeDtype...]
where the time goes in v3:
time: 19.1 us; the launch traced here: 18.9 us
  Pallas kernels  18.3 us (96%)
  between operations  0.64 us (3%)
    pallas_call x1, Pallas kernels, fused(): pl.pallas_call(functools.partial(kernel, n, m), out_shape=(jax.ShapeDtype...  16.9 us
    pallas_call x1, Pallas kernels, fused(): pl.pallas_call(finish, out_shape=(jax.ShapeDtypeStruct((ROWS, LANES), f32...  1.32 us

profile of v3, /device:TPU:0, one launch (start us, length us, event | category | flops | bytes accessed | tf_op | source)
XLA Modules:
  0.0 18.9 jit_solution(10315948823660780324)
XLA Ops:
  0.6 16.9 %shard_map.58 = (f32[8,128]{1,0:T(8,128)}, f32[1,128]{1,0:T(1,128)}, f32[16,128]{1,0:T(8,128)}) custom-call(f32[8,2048]{1,0:T(8,128)} %x_hbm.1, f32[8]{0:T(128)} %e_hbm.1, f32[16,128]{1,0:T(8,128)} %bitcast.2), custom_call_target="tpu_custom_call" | custom-call | tf_op jit(solution)/shard_map/pallas_call | solution.py:181
  17.6 1.3 %shard_map.59 = (f32[8,128]{1,0:T(8,128)}, f32[8]{0:T(128)}, f32[16,128]{1,0:T(8,128)}) custom-call(f32[8,128]{1,0:T(8,128)} %get-tuple-element.9.rows_in, f32[1,128]{1,0:T(1,128)} %get-tuple-element.10.coeffs_in, f32[16,128]{1,0:T(8,128)} %get-tuple-element.11.update_in), custom_call_target="tpu_custom_call" | custom-call | tf_op jit(solution)/shard_map/pallas_call | solution.py:206

commit v4 on v3

--- a/solution.py
+++ b/solution.py
@@ -19,7 +19,7 @@
 
 def kernel(
     n, m, x_hbm, e_hbm, p_hbm, rows_ref, coeffs_ref, update_ref,
-    x_ref, e_ref, p_ref, tiles, w_rows, y_rows, k_send, k_recv, fin,
+    x_ref, e_ref, p_ref, tiles, w_rows, y_rows, k_send, k_recv, fin, first,
     in_sem, send_sem, recv_sem,
 ):
     walkers = n * ROWS
@@ -125,6 +125,10 @@
         for c in range(chunks)
     ]
     norm = jnp.sum(t * t, axis=1, keepdims=True)
+    for c in range(chunks):
+        first[pos, :, cols(c)] = ct[c]
+    for mate in mates:
+        remote(first.at[pos], first.at[pos], 5, team + mate).start()
 
     wait_all(y_rows, m - 1, recv_sem.at[2])
     image = jnp.sum(y_rows[...], axis=0) + damping * t
@@ -140,9 +144,8 @@
         ci = jnp.sum(tiles[:, :, cols(c)].reshape(walkers, LANES) * i_col, axis=0, keepdims=True)
         bd = (bt[c] - alpha * bi) + beta * bt[c]
         squares = squares + bd * bd
-        fin[pos, :, cols(c)] = alpha * ct[c] + momentum * p_ref[pl.ds(pos * chunks + c, 1), :]
-        fin[pos, :, cols(chunks + c)] = (ct[c] - alpha * ci) + beta * ct[c]
-    fin[pos, :, cols(2 * chunks)] = squares
+        fin[pos, :, cols(c)] = (ct[c] - alpha * ci) + beta * ct[c]
+    fin[pos, :, cols(chunks)] = squares
     for mate in mates:
         remote(fin.at[pos], fin.at[pos], 4, team + mate).start()
 
@@ -150,20 +153,26 @@
     wait_all(k_recv, m - 1, recv_sem.at[3])
     rows_ref[...] = jnp.sum(k_recv[...], axis=0)
 
+    wait_all(first, m - 1, recv_sem.at[5])
+    base = [
+        alpha * first[k // chunks, :, cols(k % chunks)] + momentum * p_ref[k : k + 1, :]
+        for k in range(m * chunks)
+    ]
     wait_all(fin, m - 1, recv_sem.at[4])
-    curve = jnp.sum(jnp.sum(fin[:, :, cols(2 * chunks)], axis=0), axis=1, keepdims=True)
+    curve = jnp.sum(jnp.sum(fin[:, :, cols(chunks)], axis=0), axis=1, keepdims=True)
     alpha2 = norm_next / (curve + damping * square)
     coeffs = alpha * t + alpha2 * direction
     coeffs_ref[...] = pltpu.roll(coeffs, lax.rem(walkers - me * ROWS, walkers), 1)
     for k in range(m * chunks):
         owner, c = k // chunks, k % chunks
-        update_ref[k : k + 1, :] = fin[owner, :, cols(c)] + alpha2 * fin[owner, :, cols(chunks + c)]
+        update_ref[k : k + 1, :] = base[k] + alpha2 * fin[owner, :, cols(c)]
 
     wait_all(tiles, n - 1, send_sem.at[0])
     wait_all(w_rows, n - 1, send_sem.at[1])
     wait_all(y_rows, m - 1, send_sem.at[2])
     wait_all(k_recv, m - 1, send_sem.at[3])
     wait_all(fin, m - 1, send_sem.at[4])
+    wait_all(first, m - 1, send_sem.at[5])
 
 
 def finish(rows_in, coeffs_in, update_in, rows_ref, coeffs_ref, update_ref):
@@ -196,10 +205,11 @@
             pltpu.VMEM((m, 1, LANES), f32),
             pltpu.VMEM((m, ROWS, LANES), f32),
             pltpu.VMEM((m, ROWS, LANES), f32),
-            pltpu.VMEM((m, 1, 2 * width + LANES), f32),
+            pltpu.VMEM((m, 1, width + LANES), f32),
+            pltpu.VMEM((m, 1, width), f32),
             pltpu.SemaphoreType.DMA((3,)),
-            pltpu.SemaphoreType.DMA((5,)),
-            pltpu.SemaphoreType.DMA((5,)),
+            pltpu.SemaphoreType.DMA((6,)),
+            pltpu.SemaphoreType.DMA((6,)),
         ],
         compiler_params=pltpu.CompilerParams(collective_id=0, has_side_effects=True),
     )(log_grads, local_energy, prev_update.reshape(size // LANES, LANES))

time: 19.1 us -> 19.1 us (level)
  no operation moved by 1% of the time
where the time goes in v4:
time: 19.1 us; the launch traced here: 18.9 us
  Pallas kernels  18.3 us (96%)
  between operations  0.64 us (3%)
    pallas_call x1, Pallas kernels, fused(): pl.pallas_call(functools.partial(kernel, n, m), out_shape=(jax.ShapeDtype...  17 us
    pallas_call x1, Pallas kernels, fused(): pl.pallas_call(finish, out_shape=(jax.ShapeDtypeStruct((ROWS, LANES), f32...  1.32 us

profile of v4, /device:TPU:0, one launch (start us, length us, event | category | flops | bytes accessed | tf_op | source)
XLA Modules:
  0.0 18.9 jit_solution(7648575560754868124)
XLA Ops:
  0.6 17.0 %shard_map.58 = (f32[8,128]{1,0:T(8,128)}, f32[1,128]{1,0:T(1,128)}, f32[16,128]{1,0:T(8,128)}) custom-call(f32[8,2048]{1,0:T(8,128)} %x_hbm.1, f32[8]{0:T(128)} %e_hbm.1, f32[16,128]{1,0:T(8,128)} %bitcast.2), custom_call_target="tpu_custom_call" | custom-call | tf_op jit(solution)/shard_map/pallas_call | solution.py:190
  17.6 1.3 %shard_map.59 = (f32[8,128]{1,0:T(8,128)}, f32[8]{0:T(128)}, f32[16,128]{1,0:T(8,128)}) custom-call(f32[8,128]{1,0:T(8,128)} %get-tuple-element.9.rows_in, f32[1,128]{1,0:T(1,128)} %get-tuple-element.10.coeffs_in, f32[16,128]{1,0:T(8,128)} %get-tuple-element.11.update_in), custom_call_target="tpu_custom_call" | custom-call | tf_op jit(solution)/shard_map/pallas_call | solution.py:216
